TPU v7x, 32 devices: a whole 2x2x4 slice. The times are simulated.
32 devices in a mesh: vol: 8 (over z, y), seq: 4 (over x, core).
Axes of the slice: x: 2, y: 2, z: 4, core: 2. Of those that a mesh axis runs over, the one named last changes fastest.
Arguments:
- volume_slices: int32 [8], replicated, may hold values from 1 to 4, as said below
- volume_owner: int32 [8], replicated, may hold values from 0 to 7, as said below
- tokens: bfloat16 [32, 1024, 768], P('vol', 'seq'), may hold values from -6 to 6
- cotangent: bfloat16 [32, 1024, 768], P('vol', 'seq'), may hold values from -6 to 6
- attend_gain: bfloat16 [768], replicated, may hold values from 0.5 to 1.5
- attend_shift: bfloat16 [768], replicated, may hold values from -1 to 1
- input_weight: bfloat16 [768, 2304], replicated, may hold values from -0.3125 to 0.3125
- query_bias: bfloat16 [768], replicated, may hold values from -1 to 1
- value_bias: bfloat16 [768], replicated, may hold values from -1 to 1
- output_weight: bfloat16 [768, 768], replicated, may hold values from -0.625 to 0.625
- output_bias: bfloat16 [768], replicated, may hold values from -1 to 1
- mixer_gain: bfloat16 [768], replicated, may hold values from 0.5 to 1.5
- mixer_shift: bfloat16 [768], replicated, may hold values from -1 to 1
- expand_weight: bfloat16 [768, 3072], replicated, may hold values from -0.21875 to 0.21875
- expand_bias: bfloat16 [3072], replicated, may hold values from -1 to 1
- reduce_weight: bfloat16 [3072, 768], replicated, may hold values from -0.109375 to 0.109375
- reduce_bias: bfloat16 [768], replicated, may hold values from -1 to 1
Outputs:
- block_out: bfloat16 [32, 1024, 768], P('vol', 'seq')
- tokens_grad: float32 [32, 1024, 768], P('vol', 'seq')
- attend_gain_grad: float32 [768], P('vol')
- attend_shift_grad: float32 [768], P('vol')
- input_weight_grad: float32 [768, 2304], P('vol')
- query_bias_grad: float32 [768], P('vol')
- value_bias_grad: float32 [768], P('vol')
- output_weight_grad: float32 [768, 768], P('vol')
- output_bias_grad: float32 [768], P('vol')
- mixer_gain_grad: float32 [768], P('vol')
- mixer_shift_grad: float32 [768], P('vol')
- expand_weight_grad: float32 [768, 3072], P('vol')
- expand_bias_grad: float32 [3072], P('vol')
- reduce_weight_grad: float32 [3072, 768], P('vol')
- reduce_bias_grad: float32 [768], P('vol')
Inputs may be any that keep to these rules, and one draw needn't show every extreme that they name: `volume_slices`: each volume has 1 to 4 slices in this step. The volumes that one index of vol owns hold at most 4 slices together, and exactly 4 on some index; they fill that index's slots from the first. `volume_owner`: each index of vol owns exactly 1 volume.
All inputs are finite; a program needn't handle non-finite values.
Results may differ from a plain program's by a relative error of at most 0.017.
Values may be sent and summed in bfloat16 or wider, within the bound.
No kernel may reach another device: no remote copies, remote signals or barrier semaphores. Data moves between devices by JAX's collectives and lax.ppermute only.
A program may use at most 256 MiB of HBM per device.

v0:
```python
from functools import partial

import jax
import jax.numpy as jnp
from jax import lax
from jax.sharding import PartitionSpec as P

HEAD_DIM = 64


def from_behind(x, axis, by):
    count = lax.axis_size(axis)
    return lax.ppermute(x, axis, [(i, (i + by) % count) for i in range(count)])


def normalize(values, gain, shift):
    centre = jnp.mean(values, axis=-1, keepdims=True)
    spread = values - centre
    variance = jnp.mean(spread * spread, axis=-1, keepdims=True)
    return spread * lax.rsqrt(variance + 1e-06) * gain + shift


def split_heads(queries, keyval):
    slice_count, row_count, features = queries.shape
    head_count = features // HEAD_DIM
    key_count = keyval.shape[1]
    query_heads = queries.reshape(slice_count, row_count, head_count, HEAD_DIM)
    key_heads = keyval[:, :, :features].reshape(slice_count, key_count, head_count, HEAD_DIM)
    value_heads = keyval[:, :, features:].reshape(slice_count, key_count, head_count, HEAD_DIM)
    scores = jnp.einsum(
        "crhd,cshd->chrs", query_heads, key_heads, preferred_element_type=jnp.float32
    ) * HEAD_DIM ** (-0.5)
    return (scores, query_heads, key_heads, value_heads)


def absorb(state, queries, keyval):
    highest, summed, collected = state
    scores, query_heads, key_heads, value_heads = split_heads(queries, keyval)
    raised = jnp.maximum(highest, jnp.max(scores, axis=-1))
    shifted = jnp.exp(scores - raised[..., None])
    damping = jnp.exp(highest - raised)
    summed = summed * damping + jnp.sum(shifted, axis=-1)
    update = jnp.einsum(
        "chrs,cshd->crhd",
        shifted.astype(jnp.bfloat16),
        value_heads,
        preferred_element_type=jnp.float32,
    )
    collected = collected * jnp.swapaxes(damping, 1, 2)[..., None] + update
    return (raised, summed, collected)


def reflect(queries, keyval, logsum, grad_heads, delta):
    slice_count, row_count, features = queries.shape
    key_count = keyval.shape[1]
    scores, query_heads, key_heads, value_heads = split_heads(queries, keyval)
    weights = jnp.exp(scores - logsum[..., None])
    d_values = jnp.einsum(
        "chrs,crhd->cshd",
        weights.astype(jnp.bfloat16),
        grad_heads,
        preferred_element_type=jnp.float32,
    )
    d_weights = jnp.einsum(
        "crhd,cshd->chrs", grad_heads, value_heads, preferred_element_type=jnp.float32
    )
    d_scores = (weights * (d_weights - delta[..., None])).astype(jnp.bfloat16)
    scaling = HEAD_DIM ** (-0.5)
    d_queries = (
        jnp.einsum("chrs,cshd->crhd", d_scores, key_heads, preferred_element_type=jnp.float32)
        * scaling
    )
    d_keys = (
        jnp.einsum("chrs,crhd->cshd", d_scores, query_heads, preferred_element_type=jnp.float32)
        * scaling
    )
    d_keyval = jnp.concatenate(
        [
            d_keys.reshape(slice_count, key_count, features),
            d_values.reshape(slice_count, key_count, features),
        ],
        axis=-1,
    )
    return (d_queries.reshape(slice_count, row_count, features), d_keyval)


def on_device(
    volume_slices,
    volume_owner,
    tokens,
    cotangent,
    attend_gain,
    attend_shift,
    input_weight,
    query_bias,
    value_bias,
    output_weight,
    output_bias,
    mixer_gain,
    mixer_shift,
    expand_weight,
    expand_bias,
    reduce_weight,
    reduce_bias,
):
    slice_count, row_count, features = tokens.shape
    head_count = features // HEAD_DIM
    hidden_width = expand_weight.shape[1]
    position = lax.axis_index("vol")
    volume_load = jnp.sum(jnp.where(volume_owner == position, volume_slices, 0))
    first_slot = 0
    slot_number = jnp.arange(slice_count) + first_slot
    occupied = (slot_number < volume_load).astype(jnp.float32)[:, None, None]
    source = tokens.astype(jnp.float32)
    first, first_back = jax.vjp(
        normalize, source, attend_gain.astype(jnp.float32), attend_shift.astype(jnp.float32)
    )
    first_low = first.astype(jnp.bfloat16)
    biases = jnp.concatenate(
        [
            query_bias.astype(jnp.float32),
            jnp.zeros((features,), jnp.float32),
            value_bias.astype(jnp.float32),
        ]
    )
    packed = (jnp.dot(first_low, input_weight, preferred_element_type=jnp.float32) + biases).astype(
        jnp.bfloat16
    )
    queries = packed[:, :, :features]
    keyval = packed[:, :, features:]
    peers = lax.axis_size("seq")
    start_state = (
        jnp.full((slice_count, head_count, row_count), -jnp.inf, jnp.float32),
        jnp.zeros((slice_count, head_count, row_count), jnp.float32),
        jnp.zeros((slice_count, row_count, head_count, HEAD_DIM), jnp.float32),
    )
    state = start_state
    travelling = keyval
    for turn in range(peers):
        state = absorb(state, queries, travelling)
        if turn + 1 < peers:
            travelling = from_behind(travelling, "seq", 1)
    highest, summed, collected = state
    mixed_raw = collected / jnp.swapaxes(summed, 1, 2)[..., None]
    logsum = highest + jnp.log(summed)
    mixed_low = mixed_raw.reshape(slice_count, row_count, features).astype(jnp.bfloat16)
    middle = (
        source
        + jnp.dot(mixed_low, output_weight, preferred_element_type=jnp.float32)
        + output_bias.astype(jnp.float32)
    )
    second, second_back = jax.vjp(
        normalize, middle, mixer_gain.astype(jnp.float32), mixer_shift.astype(jnp.float32)
    )
    second_low = second.astype(jnp.bfloat16)
    hidden = jnp.dot(
        second_low, expand_weight, preferred_element_type=jnp.float32
    ) + expand_bias.astype(jnp.float32)
    activated, gelu_back = jax.vjp(partial(jax.nn.gelu, approximate=False), hidden)
    activated_low = activated.astype(jnp.bfloat16)
    final = (
        middle
        + jnp.dot(activated_low, reduce_weight, preferred_element_type=jnp.float32)
        + reduce_bias.astype(jnp.float32)
    )
    block_out = (final * occupied).astype(jnp.bfloat16)
    upstream = (cotangent.astype(jnp.float32) * occupied).astype(jnp.bfloat16)
    reduce_grad = jnp.einsum(
        "crf,crd->fd", activated_low, upstream, preferred_element_type=jnp.float32
    )
    reduce_bias_grad = jnp.sum(upstream.astype(jnp.float32), axis=(0, 1))
    d_activated = jnp.einsum(
        "crd,fd->crf", upstream, reduce_weight, preferred_element_type=jnp.float32
    )
    (d_hidden,) = gelu_back(d_activated)
    d_hidden_low = d_hidden.astype(jnp.bfloat16)
    expand_grad = jnp.einsum(
        "crd,crf->df", second_low, d_hidden_low, preferred_element_type=jnp.float32
    )
    expand_bias_grad = jnp.sum(d_hidden_low.astype(jnp.float32), axis=(0, 1))
    d_second = jnp.einsum(
        "crf,df->crd", d_hidden_low, expand_weight, preferred_element_type=jnp.float32
    )
    d_middle_norm, mixer_gain_grad, mixer_shift_grad = second_back(d_second)
    d_middle = upstream.astype(jnp.float32) + d_middle_norm
    d_branch = d_middle.astype(jnp.bfloat16)
    output_grad = jnp.einsum("cri,crj->ij", mixed_low, d_branch, preferred_element_type=jnp.float32)
    output_bias_grad = jnp.sum(d_branch.astype(jnp.float32), axis=(0, 1))
    d_mixed = jnp.einsum(
        "crj,ij->cri", d_branch, output_weight, preferred_element_type=jnp.float32
    ).astype(jnp.bfloat16)
    grad_heads = d_mixed.reshape(slice_count, row_count, head_count, HEAD_DIM)
    delta = jnp.swapaxes(jnp.sum(grad_heads.astype(jnp.float32) * mixed_raw, axis=-1), 1, 2)
    travelling = keyval
    owed = jnp.zeros((slice_count, row_count, 2 * features), jnp.float32)
    d_queries = jnp.zeros((slice_count, row_count, features), jnp.float32)
    for turn in range(peers):
        part_queries, part_keyval = reflect(queries, travelling, logsum, grad_heads, delta)
        d_queries = d_queries + part_queries
        owed = from_behind((owed + part_keyval).astype(jnp.bfloat16), "seq", 1).astype(jnp.float32)
        if turn + 1 < peers:
            travelling = from_behind(travelling, "seq", 1)
    d_packed = jnp.concatenate([d_queries, owed], axis=-1).astype(jnp.bfloat16)
    input_grad = jnp.einsum("cri,crj->ij", first_low, d_packed, preferred_element_type=jnp.float32)
    bias_rows = jnp.sum(d_packed.astype(jnp.float32), axis=(0, 1))
    query_bias_grad = bias_rows[:features]
    value_bias_grad = bias_rows[2 * features :]
    d_first = jnp.einsum("crj,ij->cri", d_packed, input_weight, preferred_element_type=jnp.float32)
    d_source, attend_gain_grad, attend_shift_grad = first_back(d_first)
    tokens_grad = d_middle + d_source
    vectors = jnp.concatenate(
        [
            jnp.stack(
                [
                    attend_gain_grad,
                    attend_shift_grad,
                    query_bias_grad,
                    value_bias_grad,
                    output_bias_grad,
                    mixer_gain_grad,
                    mixer_shift_grad,
                    reduce_bias_grad,
                ],
                axis=1,
            ),
            expand_bias_grad.reshape(features, hidden_width // features),
        ],
        axis=1,
    )
    parts = (
        lax.psum_scatter(input_grad, "vol", scatter_dimension=0, tiled=True),
        lax.psum_scatter(output_grad, "vol", scatter_dimension=0, tiled=True),
        lax.psum_scatter(expand_grad, "vol", scatter_dimension=0, tiled=True),
        lax.psum_scatter(reduce_grad, "vol", scatter_dimension=0, tiled=True),
        lax.psum_scatter(vectors, "vol", scatter_dimension=0, tiled=True),
    )
    totals = (
        lax.psum(parts[0].astype(jnp.bfloat16), "seq").astype(jnp.float32),
        lax.psum(parts[1].astype(jnp.bfloat16), "seq").astype(jnp.float32),
        lax.psum(parts[2].astype(jnp.bfloat16), "seq").astype(jnp.float32),
        lax.psum(parts[3].astype(jnp.bfloat16), "seq").astype(jnp.float32),
        lax.psum(parts[4].astype(jnp.bfloat16), "seq").astype(jnp.float32),
    )
    input_total, output_total, expand_total, reduce_total, vector_total = totals
    return (
        block_out,
        tokens_grad,
        vector_total[:, 0],
        vector_total[:, 1],
        input_total,
        vector_total[:, 2],
        vector_total[:, 3],
        output_total,
        vector_total[:, 4],
        vector_total[:, 5],
        vector_total[:, 6],
        expand_total,
        vector_total[:, 8:].reshape(-1),
        reduce_total,
        vector_total[:, 7],
    )


def solution(mesh):
    placed = (
        P(),
        P(),
        P("vol", "seq", None),
        P("vol", "seq", None),
        P(),
        P(),
        P(),
        P(),
        P(),
        P(),
        P(),
        P(),
        P(),
        P(),
        P(),
        P(),
        P(),
    )
    return jax.shard_map(
        on_device,
        mesh=mesh,
        in_specs=placed,
        out_specs=(
            P("vol", "seq", None),
            P("vol", "seq", None),
            P("vol"),
            P("vol"),
            P("vol", None),
            P("vol"),
            P("vol"),
            P("vol", None),
            P("vol"),
            P("vol"),
            P("vol"),
            P("vol", None),
            P("vol"),
            P("vol", None),
            P("vol"),
        ),
        check_vma=False,
    )
```

profile of v0, /device:TPU:0, one launch (start us, length us, event | category | flops | bytes accessed | tf_op | source)
XLA Modules:
  0.0 949.8 jit_solution(13724537801954838839)
XLA Ops:
  21.9 37.0 %collective-permute-done = bf16[4,256,1536]{2,1,0:T(8,128)(2,1)} collective-permute-done((bf16[4,256,1536]{2,1,0:T(8,128)(2,1)S(1)}, bf16[4,256,1536]{2,1,0:T(8,128)(2,1)}, u32[]{:S(2)}, u32[]{:S(2)}) %collective-permute-start) | collective-permute-done | bytes 3145760 | tf_op jit(solution)/shard_map/ppermute | solution.py:13
  75.7 20.2 %collective-permute-done.1 = bf16[4,256,1536]{2,1,0:T(8,128)(2,1)} collective-permute-done((bf16[4,256,1536]{2,1,0:T(8,128)(2,1)}, bf16[4,256,1536]{2,1,0:T(8,128)(2,1)}, u32[]{:S(2)}, u32[]{:S(2)}) %collective-permute-start.1) | collective-permute-done | bytes 3145760 | tf_op jit(solution)/shard_map/ppermute | solution.py:13
  114.8 8.9 multiply_reduce_fusion.2
  132.7 8.9 multiply_reduce_fusion.1
  150.6 9.5 multiply_reduce_fusion
  178.0 17.3 %fusion.6 = (f32[4,12,256]{2,1,0:T(8,128)S(1)}, f32[4,12,256]{2,1,0:T(8,128)S(1)}) fusion(f32[4,12,256,256]{2,3,1,0:T(8,128)S(1)} %bitcast.234, f32[4,12,256]{2,1,0:T(8,128)S(1)} %copy-done.42, f32[4,12,256]{2,1,0:T(8,128)S(1)} %copy-done.47, f32[4,12,256,256]{2,3,1,0:T(8,128)} %get-tuple-element.64), kind=kLoop, calls=%fused_computation.34 | loop fusion | flops 18849792 | bytes 25362432 | tf_op jit(solution)/shard_map/reduce_sum | solution.py:42
  195.5 10.0 %fusion.126 = (bf16[4,256,12,64]{1,3,2,0:T(8,128)(2,1)}, f32[4,256,12,64]{1,3,2,0:T(8,128)}) fusion(f32[4,256,12]{1,2,0:T(8,128)S(1)} %get-tuple-element.34, bf16[4,256,12,64]{1,3,2,0:T(8,128)(2,1)S(1)} %bitcast.274, f32[4,12,256,256]{2,3,1,0:T(8,128)} %get-tuple-element.64, f32[4,12,256]{2,1,0:T(8,128)S(1)} %copy-done.47, ...), kind=kOutput, calls=%fused_computation.205 | convolution fusion | flops 419168256 | bytes 28606464 | tf_op jit(solution)/shard_map/chrs,cshd->crhd/dot_general | solution.py:43
  209.6 11.4 %fusion.80 = (u8[256,3072]{1,0:T(8,128)(4,1)S(1)}, u8[256,3072]{1,0:T(8,128)(4,1)S(1)}, f32[4,256,3072]{2,1,0:T(8,128)S(1)}) fusion(f32[3072]{0:T(1024)S(1)} %copy-done.61, bf16[768,3072]{1,0:T(8,128)(2,1)} %param.30, f32[4,256,768]{2,1,0:T(8,128)S(1)} %get-tuple-element.74, f32[768]{0:T(1024)S(1)} %convert_element_type.191, ...), kind=kOutput, calls=%fused_computation.136 | convolution fusion | flops 4878237696 | bytes 22046720 | tf_op jit(solution)/shard_map/dot_general | solution.py:156
  221.1 30.3 %multiply_convert_fusion.4 = (bf16[4,256,3072]{2,1,0:T(8,128)(2,1)}, f32[4,256,3072]{2,1,0:T(8,128)}) fusion(f32[4,256,3072]{2,1,0:T(8,128)S(1)} %get-tuple-element.75, f32[3072]{0:T(1024)S(1)} %copy-done.61, u8[256,3072]{1,0:T(8,128)(4,1)S(1)} %get-tuple-element.16, u8[256,3072]{1,0:T(8,128)(4,1)S(1)} %get-tuple-element.15), kind=kLoop, calls=%fused_computation.17 | loop fusion | flops 223346688 | bytes 33042432 | tf_op jit(solution)/shard_map/convert_element_type | solution.py:160
  251.4 18.8 %convert_reduce_fusion = (f32[3072]{0:T(1024)}, bf16[4,256,3072]{2,1,0:T(8,128)(2,1)}) fusion(f32[4,256,3072]{2,1,0:T(8,128)} %get-tuple-element.33, bf16[3072,768]{1,0:T(8,128)(2,1)} %param.32, bf16[4,256,768]{2,1,0:T(8,128)(2,1)} %param.20, f32[4]{0:T(128)S(1)} %copy-done.78, f32[4,256,3072]{2,1,0:T(8,128)} %copy-done.32, f32[3072]{0:T(1024)S(1)} %copy-done.61), kind=kOutput, calls=%fused_computation.7 | convolution fusion | flops 4887671808 | bytes 37773328 | tf_op jit(solution)/shard_map/crd,fd->crf/dot_general | solution.py:172
  270.3 9.8 %multiply_reduce_fusion.4 = (f32[768]{0:T(1024)}, f32[4,256]{1,0:T(4,128)S(1)}, f32[768]{0:T(1024)}, f32[4,256,768]{2,1,0:T(8,128)S(1)}) fusion(f32[4,256,768]{2,1,0:T(8,128)S(1)} %get-tuple-element.74, f32[4,256]{1,0:T(4,128)S(1)} %fusion.102, f32[4,256]{1,0:T(4,128)S(1)} %broadcast_multiply_fusion, f32[768]{0:T(1024)S(1)} %convert_element_type.190, ...), kind=kOutput, calls=%fused_computation.125 | convolution fusion | flops 4838126592 | bytes 17323008 | tf_op jit(solution)/shard_map/crf,df->crd/dot_general | solution.py:181
  287.2 10.3 %convolution_bitcast_fusion = f32[3072,768]{1,0:T(8,128)} fusion(bf16[4,256,3072]{2,1,0:T(8,128)(2,1)} %get-tuple-element.32, bf16[4,256,768]{2,1,0:T(8,128)(2,1)} %param.20, f32[4]{0:T(128)} %compare_convert_fusion), kind=kOutput, calls=%fused_computation.82 | convolution fusion | flops 4834197504 | bytes 17301520 | tf_op jit(solution)/shard_map/crf,crd->fd/dot_general | solution.py:168
  297.6 11.1 %convolution_bitcast_fusion.1 = f32[768,3072]{1,0:T(8,128)} fusion(bf16[4,256,3072]{2,1,0:T(8,128)(2,1)} %get-tuple-element.79, f32[4,256,768]{2,1,0:T(8,128)} %copy-done.14, f32[768]{0:T(1024)S(1)} %convert_element_type.191, f32[768]{0:T(1024)S(1)} %convert_element_type.190, f32[4,256]{1,0:T(4,128)S(1)} %fusion.102, f32[4,256]{1,0:T(4,128)S(1)} %broadcast_multiply_fusion), kind=kOutput, calls=%fused_computation.83 | convolution fusion | flops 4835770368 | bytes 18888704 | tf_op jit(solution)/shard_map/crd,crf->df/dot_general | solution.py:177
  317.1 8.7 fusion.86
  363.9 9.6 %multiply_convert_fusion.2 = bf16[4,12,256,256]{2,3,1,0:T(8,128)(2,1)S(1)} fusion(f32[4,12,256,256]{2,3,1,0:T(8,128)} %get-tuple-element.70, f32[4,12,256]{2,1,0:T(8,128)} %bitcast.282, f32[4,12,256]{2,1,0:T(8,128)} %copy-done.36, bf16[4,256,12,64]{1,3,2,0:T(8,128)(2,1)} %bitcast.245, bf16[4,256,12,64]{1,3,2,0:T(8,128)(2,1)} %bitcast.271), kind=kOutput, calls=%fused_computation.12 | convolution fusion | flops 418381824 | bytes 22118400 | tf_op jit(solution)/shard_map/crhd,cshd->chrs/dot_general | solution.py:64
  405.3 9.1 multiply_convert_fusion.1
  448.7 9.0 multiply_convert_fusion
  496.0 20.5 %collective-permute-done.6 = bf16[4,256,1536]{2,1,0:T(8,128)(2,1)} collective-permute-done((bf16[4,256,1536]{2,1,0:T(8,128)(2,1)}, bf16[4,256,1536]{2,1,0:T(8,128)(2,1)}, u32[]{:S(2)}, u32[]{:S(2)}) %collective-permute-start.6) | collective-permute-done | bytes 3145760 | tf_op jit(solution)/shard_map/ppermute | solution.py:13
  516.5 9.9 %convolution_bitcast_fusion.2 = f32[768,2304]{1,0:T(8,128)} fusion(bf16[4,256,1536]{2,1,0:T(8,128)(2,1)} %collective-permute-done.6, bf16[4,256,768]{2,1,0:T(8,128)(2,1)} %copy.268, bf16[4,256,768]{2,1,0:T(8,128)(2,1)} %param.19, f32[768]{0:T(1024)S(1)} %copy-done.75, f32[768]{0:T(1024)S(1)} %copy-done.63, f32[4,256]{1,0:T(4,128)S(1)} %copy-done.66, ...), kind=kOutput, calls=%fused_computation.84 | convolution fusion | flops 3638034432 | bytes 13383680 | tf_op jit(solution)/shard_map/cri,crj->ij/dot_general | solution.py:204
  558.5 132.2 %reduce-scatter.12.cloned.1.call-done = f32[96,3072]{1,0:T(8,128)} async-done(((f32[768,3072]{1,0:T(8,128)}), f32[96,3072]{1,0:T(8,128)}) %reduce-scatter.12.cloned.1.call-update) | async-done | bytes 1179664 | tf_op jit(solution)/shard_map/reduce_scatter | solution.py:233
  692.9 129.5 %reduce-scatter.8.cloned.1.call-done = f32[96,2304]{1,0:T(8,128)} async-done(((f32[768,2304]{1,0:T(8,128)}), f32[96,2304]{1,0:T(8,128)}) %reduce-scatter.8.cloned.1.call-update) | async-done | bytes 884752 | tf_op jit(solution)/shard_map/reduce_scatter | solution.py:231
  824.4 9.9 %multiply_convert_fusion.8 = bf16[4,256,768]{2,1,0:T(8,128)(2,1)} fusion(f32[4,256,768]{2,1,0:T(8,128)} %copy-done.14, bf16[4,256,3072]{2,1,0:T(8,128)(2,1)} %get-tuple-element.32, bf16[3072,768]{1,0:T(8,128)(2,1)} %param.32, f32[4]{0:T(128)S(1)} %copy-done.81, f32[768]{0:T(1024)S(1)} %convert_element_type.195), kind=kOutput, calls=%fused_computation.132 | convolution fusion | flops 4834983936 | bytes 15731728 | tf_op jit(solution)/shard_map/dot_general | solution.py:163
  834.3 52.0 %reduce-scatter.16.cloned.1.call-done = f32[96,12]{1,0:T(8,128)} async-done(((f32[768,12]{1,0:T(8,128)}), f32[96,12]{1,0:T(8,128)}) %reduce-scatter.16.cloned.1.call-update) | async-done | bytes 4624
  895.6 40.2 %all-reduce.3.cloned.1.call-done = (bf16[96,2304]{1,0:T(8,128)(2,1)}, bf16[96,768]{1,0:T(8,128)(2,1)}, bf16[96,3072]{1,0:T(8,128)(2,1)}, bf16[384,768]{1,0:T(8,128)(2,1)}) async-done(((bf16[96,2304]{1,0:T(8,128)(2,1)}, bf16[96,768]{1,0:T(8,128)(2,1)}, bf16[96,3072]{1,0:T(8,128)(2,1)}, bf16[384,768]{1,0:T(8,128)(2,1)}), (bf16[96,2304]{1,0:T(8,128)(2,1)}, bf16[96,768]{1,0:T(8,128)(2,1)}, ...) | async-done | bytes 1769488 | tf_op jit(solution)/shard_map/psum | solution.py:238
  (335 shorter events, 300.3 us)
Async XLA Ops:
  7.2 547.5 %reduce-scatter.10.cloned.1.call-start = ((), (), s32[]{:S(2)}) async-start(), calls=%async_computation.6 | async-start | bytes 2654208 | tf_op jit(solution)/shard_map/reduce_scatter | solution.py:232
  19.4 39.5 %copy-start.77 = (bf16[768]{0:T(1024)(128)(2,1)S(1)}, bf16[768]{0:T(1024)(128)(2,1)}, u32[]{:S(2)}) copy-start(bf16[768]{0:T(1024)(128)(2,1)} %param.28) | copy-start | bytes 4612
  19.4 41.5 %copy-start.73 = (bf16[3072]{0:T(1024)(128)(2,1)S(1)}, bf16[3072]{0:T(1024)(128)(2,1)}, u32[]{:S(2)}) copy-start(bf16[3072]{0:T(1024)(128)(2,1)} %param.31) | copy-start | bytes 18436
  21.5 37.4 %collective-permute-start = (bf16[4,256,1536]{2,1,0:T(8,128)(2,1)S(1)}, bf16[4,256,1536]{2,1,0:T(8,128)(2,1)}, u32[]{:S(2)}, u32[]{:S(2)}) collective-permute-start(bf16[4,256,1536]{2,1,0:T(8,128)(2,1)S(1)} %slice.97), channel_id=1, source_target_pairs={{0,1},{1,2},{2,3},{3,0},{4,5},{5,6},{6,7},{7,4},{8,9},{9,10},{10,1... | collective-permute-start | bytes 9437192 | tf_op jit(solution)/shard_map/ppermute | solution.py:13
  58.9 37.0 %collective-permute-start.1 = (bf16[4,256,1536]{2,1,0:T(8,128)(2,1)}, bf16[4,256,1536]{2,1,0:T(8,128)(2,1)}, u32[]{:S(2)}, u32[]{:S(2)}) collective-permute-start(bf16[4,256,1536]{2,1,0:T(8,128)(2,1)} %collective-permute-done), channel_id=1, source_target_pairs={{0,1},{1,2},{2,3},{3,0},{4,5},{5,6},{6,7},{7,4},{8,9},{9,10},{10,1... | collective-permute-start | bytes 9437192 | tf_op jit(solution)/shard_map/ppermute | solution.py:13
  95.9 45.7 %collective-permute-start.2 = (bf16[4,256,1536]{2,1,0:T(8,128)(2,1)}, bf16[4,256,1536]{2,1,0:T(8,128)(2,1)}, u32[]{:S(2)}, u32[]{:S(2)}) collective-permute-start(bf16[4,256,1536]{2,1,0:T(8,128)(2,1)} %collective-permute-done.1), channel_id=1, source_target_pairs={{0,1},{1,2},{2,3},{3,0},{4,5},{5,6},{6,7},{7,4},{8,9},{9,10},{10,1... | collective-permute-start | bytes 9437192 | tf_op jit(solution)/shard_map/ppermute | solution.py:13
  178.0 17.5 %copy-start.20 = (f32[4,12,64,256]{3,2,1,0:T(8,128)S(1)}, f32[4,12,64,256]{3,2,1,0:T(8,128)}, u32[]{:S(2)}) copy-start(f32[4,12,64,256]{3,2,1,0:T(8,128)} %fusion.32) | copy-start | bytes 9437188
  208.9 71.2 %copy-start.14 = (f32[4,256,768]{2,1,0:T(8,128)}, f32[4,256,768]{2,1,0:T(8,128)S(1)}, u32[]{:S(2)}) copy-start(f32[4,256,768]{2,1,0:T(8,128)S(1)} %get-tuple-element.74) | copy-start | bytes 9437188
  221.0 30.4 %copy-start.32 = (f32[4,256,3072]{2,1,0:T(8,128)}, f32[4,256,3072]{2,1,0:T(8,128)S(1)}, u32[]{:S(2)}) copy-start(f32[4,256,3072]{2,1,0:T(8,128)S(1)} %get-tuple-element.75) | copy-start | bytes 37748740
  221.1 30.4 %copy-start.78 = (f32[4]{0:T(128)S(1)}, f32[4]{0:T(128)}, u32[]{:S(2)}) copy-start(f32[4]{0:T(128)} %compare_convert_fusion) | copy-start | bytes 52
  287.1 269.2 %reduce-scatter.14.cloned.1.call-start = ((), (), s32[]{:S(2)}) async-start(), calls=%async_computation.8 | async-start | bytes 10616832 | tf_op jit(solution)/shard_map/reduce_scatter | solution.py:234
  297.6 393.2 %reduce-scatter.12.cloned.1.call-start = ((), (), s32[]{:S(2)}) async-start(), calls=%async_computation.7 | async-start | bytes 10616832 | tf_op jit(solution)/shard_map/reduce_scatter | solution.py:233
  308.7 513.7 %reduce-scatter.8.cloned.1.call-start = ((), (), s32[]{:S(2)}) async-start(), calls=%async_computation.5 | async-start | bytes 7962624 | tf_op jit(solution)/shard_map/reduce_scatter | solution.py:231
  349.3 37.0 %collective-permute-start.3 = (bf16[4,256,1536]{2,1,0:T(8,128)(2,1)}, bf16[4,256,1536]{2,1,0:T(8,128)(2,1)}, u32[]{:S(2)}, u32[]{:S(2)}) collective-permute-start(bf16[4,256,1536]{2,1,0:T(8,128)(2,1)} %pad_maximum_fusion.1), channel_id=1, source_target_pairs={{0,1},{1,2},{2,3},{3,0},{4,5},{5,6},{6,7},{7,4},{8,9},{9,10},{10,1... | collective-permute-start | bytes 9437192 | tf_op jit(solution)/shard_map/ppermute | solution.py:13
  392.7 37.0 %collective-permute-start.4 = (bf16[4,256,1536]{2,1,0:T(8,128)(2,1)}, bf16[4,256,1536]{2,1,0:T(8,128)(2,1)}, u32[]{:S(2)}, u32[]{:S(2)}) collective-permute-start(bf16[4,256,1536]{2,1,0:T(8,128)(2,1)} %fusion.34), channel_id=1, source_target_pairs={{0,1},{1,2},{2,3},{3,0},{4,5},{5,6},{6,7},{7,4},{8,9},{9,10},{10,1... | collective-permute-start | bytes 9437192 | tf_op jit(solution)/shard_map/ppermute | solution.py:13
  436.1 37.0 %collective-permute-start.5 = (bf16[4,256,1536]{2,1,0:T(8,128)(2,1)}, bf16[4,256,1536]{2,1,0:T(8,128)(2,1)}, u32[]{:S(2)}, u32[]{:S(2)}) collective-permute-start(bf16[4,256,1536]{2,1,0:T(8,128)(2,1)} %fusion.35), channel_id=1, source_target_pairs={{0,1},{1,2},{2,3},{3,0},{4,5},{5,6},{6,7},{7,4},{8,9},{9,10},{10,1... | collective-permute-start | bytes 9437192 | tf_op jit(solution)/shard_map/ppermute | solution.py:13
  479.5 37.0 %collective-permute-start.6 = (bf16[4,256,1536]{2,1,0:T(8,128)(2,1)}, bf16[4,256,1536]{2,1,0:T(8,128)(2,1)}, u32[]{:S(2)}, u32[]{:S(2)}) collective-permute-start(bf16[4,256,1536]{2,1,0:T(8,128)(2,1)} %fusion.36), channel_id=1, source_target_pairs={{0,1},{1,2},{2,3},{3,0},{4,5},{5,6},{6,7},{7,4},{8,9},{9,10},{10,1... | collective-permute-start | bytes 9437192 | tf_op jit(solution)/shard_map/ppermute | solution.py:13
  493.2 23.3 %copy-start.60 = (f32[4,256]{1,0:T(4,128)S(1)}, f32[4,256]{1,0:T(4,128)}, u32[]{:S(2)}) copy-start(f32[4,256]{1,0:T(4,128)} %copy-done.59) | copy-start | bytes 12292
  493.2 23.3 %copy-start.63 = (f32[768]{0:T(1024)S(1)}, f32[768]{0:T(1024)}, u32[]{:S(2)}) copy-start(f32[768]{0:T(1024)} %copy-done.62) | copy-start | bytes 9220
  493.2 23.3 %copy-start.66 = (f32[4,256]{1,0:T(4,128)S(1)}, f32[4,256]{1,0:T(4,128)}, u32[]{:S(2)}) copy-start(f32[4,256]{1,0:T(4,128)} %copy-done.65) | copy-start | bytes 12292
  493.2 23.3 %copy-start.75 = (f32[768]{0:T(1024)S(1)}, f32[768]{0:T(1024)}, u32[]{:S(2)}) copy-start(f32[768]{0:T(1024)} %copy-done.74) | copy-start | bytes 9220
  526.5 359.8 %reduce-scatter.16.cloned.1.call-start = ((), (), s32[]{:S(2)}) async-start(), calls=%async_computation.9 | async-start | bytes 442368
  553.9 381.8 %all-reduce.3.cloned.1.call-start = ((), (), s32[]{:S(2)}) async-start(), calls=%async_computation.10 | async-start | bytes 3538944 | tf_op jit(solution)/shard_map/psum | solution.py:238
  556.3 268.1 %copy-start.81 = (f32[4]{0:T(128)S(1)}, f32[4]{0:T(128)}, u32[]{:S(2)}) copy-start(f32[4]{0:T(128)} %compare_convert_fusion) | copy-start | bytes 52
  (86 other events, 626.4 us)
Sparse Core Ops, SparseCore 0:
  287.3 71.5 reduce-scatter.9
  362.4 162.2 reduce-scatter.13
  528.3 162.3 reduce-scatter.11
  694.2 128.1 reduce-scatter.7
  825.9 60.3 reduce-scatter.15
  890.1 45.6 all-reduce.2
where the time goes:
time: 959 us; the launch traced here: 950 us
  waiting for transfers between devices  453 us (47%)
  matrix products  252 us (26%)
  other arithmetic  120 us (13%)
  local copies, waits for them, and re-layouts  100 us (10%)
  between operations  15.3 us (2%)
    reduce_scatter x1, waiting for transfers between devices, on_device(): lax.psum_scatter(expand_grad, 'vol', scatter_dimension=0, tiled=True)  132 us
    reduce_scatter x1, waiting for transfers between devices, on_device(): lax.psum_scatter(input_grad, 'vol', scatter_dimension=0, tiled=True)  130 us
    ppermute x7, waiting for transfers between devices, from_behind(): return lax.ppermute(x, axis, [(i, (i + by) % count) for i in range(count)])  99.2 us
    unnamed x7, waiting for transfers between devices  52.1 us
    psum x1, waiting for transfers between devices, on_device(): lax.psum(parts[0].astype(jnp.bfloat16), 'seq').astype(jnp.float32)  40.2 us
    dot_general x4, matrix products, reflect(): jnp.einsum('crhd,cshd->chrs', grad_heads, value_heads, preferred_element_...  35 us
    dot_general x4, matrix products, reflect(): jnp.einsum('chrs,crhd->cshd', weights.astype(jnp.bfloat16), grad_heads, p...  34.6 us
    dot_general x4, matrix products, split_heads(): jnp.einsum('crhd,cshd->chrs', query_heads, key_heads, preferred_element_t...  31.1 us
  transfers between devices with their start and end apart: 13, of which 10 were waited for; matrix products, arithmetic and copies ran while one was open for 32% of the time, Pallas kernels for 0%

commit v1 on v0

v1 whole, which is shorter than its diff:
```python
import functools

import jax
import jax.numpy as jnp
from jax import lax
from jax.experimental import pallas as pl
from jax.experimental.pallas import tpu as pltpu
from jax.sharding import PartitionSpec as P

HEAD_DIM = 64
PAIR = 2 * HEAD_DIM
LOG2E = 1.4426950408889634
BF = jnp.bfloat16
F32 = jnp.float32
NN = (((1,), (0,)), ((), ()))
NT = (((1,), (1,)), ((), ()))
TAIL = (
    0.11962928008603971,
    0.12075423895539067,
    0.09991176086876633,
    0.12856720585766357,
    -0.05369390237929985,
    0.20636430391507077,
    -0.15720912816414995,
    0.03567616760586865,
)


def dot(a, b, dims):
    return lax.dot_general(a, b, dims, preferred_element_type=F32)


def params():
    return pltpu.CompilerParams(vmem_limit_bytes=60 << 20)


def shape(dims, dtype=BF):
    return jax.ShapeDtypeStruct(dims, dtype)


def normal(h):
    a = jnp.abs(h)
    t = 1.0 / (1.0 + 0.3 * a)
    s = TAIL[7] * t + TAIL[6]
    for c in TAIL[5::-1]:
        s = s * t + c
    e = jnp.exp2(h * h * (-0.5 * LOG2E))
    tail = s * t * e
    return jnp.where(h >= 0, 1.0 - tail, tail), e * 0.3989422804014327


def stats(v):
    spread = v - jnp.mean(v, axis=-1, keepdims=True)
    return spread, lax.rsqrt(jnp.mean(spread * spread, axis=-1, keepdims=True) + 1e-6)


def in_kernel(x_ref, g_ref, b_ref, w_ref, bias_ref, *rest):
    x_out, first_t, packed = rest[-3:]
    x = x_ref[...]
    spread, r = stats(x.astype(F32))
    f = (spread * r * g_ref[...] + b_ref[...]).astype(BF)
    x_out[...] = x
    first_t[...] = f.T
    packed[...] = (dot(f, w_ref[...], NN) + bias_ref[...]).astype(BF)


def project_in(parts, offset, total, before, gain, shift, weight, bias):
    rows, d = parts.shape
    wide = weight.shape[1]
    tm = 256
    first_block = offset // tm

    def full(*s):
        return pl.BlockSpec(s, lambda i: (0, 0))

    in_specs = [pl.BlockSpec((tm, d), lambda i: (i, 0)), full(1, d), full(1, d), full(d, wide), full(1, wide)]
    args = [parts, gain, shift, weight, bias]
    aliases = {}
    if before is not None:
        aliases = {5: 0, 6: 1, 7: 2}
        in_specs += [pl.BlockSpec(memory_space=pl.ANY)] * 3
        args += list(before)
    return pl.pallas_call(
        in_kernel,
        grid=(rows // tm,),
        in_specs=in_specs,
        out_specs=[
            pl.BlockSpec((tm, d), lambda i: (i + first_block, 0)),
            pl.BlockSpec((d, tm), lambda i: (0, i + first_block)),
            pl.BlockSpec((tm, wide), lambda i: (i + first_block, 0)),
        ],
        out_shape=[shape((total, d)), shape((d, total)), shape((total, wide))],
        input_output_aliases=aliases,
        compiler_params=params(),
        cost_estimate=pl.CostEstimate(flops=2 * rows * d * wide, bytes_accessed=2 * (d * wide + rows * (wide + 3 * d)), transcendentals=0),
        name="project_in",
    )(*args)


def attend_kernel(q_ref, k_ref, v_ref, o_ref, inv_ref, p_ref, vx_ref, *, tq):
    n = k_ref.shape[0]
    vx_ref[:, :PAIR] = v_ref[...]
    vx_ref[:, PAIR:] = jnp.ones((n, PAIR), BF)
    low = lax.broadcasted_iota(jnp.int32, (tq, PAIR), 1) < HEAD_DIM
    for t in range(n // tq):
        rows = pl.ds(t * tq, tq)
        q = q_ref[rows, :]
        zero = jnp.zeros_like(q)
        outs = []
        for a in range(2):
            qa = jnp.where(low, q, zero) if a == 0 else jnp.where(low, zero, q)
            s = dot(qa, k_ref[...], NT)
            top = jnp.max(s, axis=-1, keepdims=True)
            p = jnp.exp2((s - top) * (LOG2E * HEAD_DIM**-0.5)).astype(BF)
            p_ref[a, rows, :] = p
            both = dot(p, vx_ref[...], NN)
            inv = 1.0 / both[:, PAIR:]
            outs.append((both[:, :PAIR] * inv, inv))
        o_ref[rows, :] = jnp.where(low, outs[0][0], outs[1][0]).astype(BF)
        inv_ref[rows, :] = jnp.where(low, outs[0][1], outs[1][1])


def attend(packed):
    n, w = packed.shape
    d = w // 3
    hp = d // PAIR

    def cols(off):
        return pl.BlockSpec((n, PAIR), lambda h: (0, h + off))

    return pl.pallas_call(
        functools.partial(attend_kernel, tq=128),
        grid=(hp,),
        in_specs=[cols(0), cols(hp), cols(2 * hp)],
        out_specs=[cols(0), cols(0), pl.BlockSpec((2, n, n), lambda h: (h, 0, 0))],
        out_shape=[shape((n, d)), shape((n, d), F32), shape((2 * hp, n, n))],
        scratch_shapes=[pltpu.VMEM((n, 2 * PAIR), BF)],
        compiler_params=params(),
        cost_estimate=pl.CostEstimate(flops=16 * n * n * d, bytes_accessed=4 * n * n * hp, transcendentals=0),
        name="attend",
    )(packed, packed, packed)


def mlp_kernel(
    c_ref, x_ref, mix_ref, li_ref, up_ref, wo_ref, bo_ref, g2_ref, s2_ref, w1_ref, b1_ref, w2_ref, b2_ref,
    out_ref, dbr_ref, do_ref, dwo_k_ref, dwo_s_ref, dw1_k_ref, dw1_s_ref, dw2_k_ref, dw2_s_ref, vec_ref, db1_ref,
    sec, sec_t, up_t, mid, dsec, acc, act, dh, *, tm, nj,
):
    j = pl.program_id(0)
    n, d = x_ref.shape
    tiles = n // tm
    c = c_ref[0]

    @pl.when(j == 0)
    def _():
        for t in range(tiles):
            rows = pl.ds(t * tm, tm)
            m = x_ref[rows, :].astype(F32) + dot(mix_ref[rows, :], wo_ref[...], NN) + bo_ref[...]
            mid[rows, :] = m
            spread, r = stats(m)
            s = (spread * r * g2_ref[...] + s2_ref[...]).astype(BF)
            sec[rows, :] = s
            sec_t[:, rows] = s.T
            up_t[:, rows] = up_ref[rows, :].T
        vec_ref[...] = jnp.zeros_like(vec_ref)

    db1 = None
    for t in range(tiles):
        rows = pl.ds(t * tm, tm)
        h = dot(sec[rows, :], w1_ref[...], NN) + b1_ref[...]
        da = dot(up_ref[rows, :], w2_ref[...], NT)
        cdf, pdf = normal(h)
        a = (h * cdf).astype(BF)
        dhv = (da * (cdf + h * pdf)).astype(BF)
        act[rows, :] = a
        dh[rows, :] = dhv
        o = dot(a, w2_ref[...], NN)
        ds = dot(dhv, w1_ref[...], NT)
        part = jnp.sum(dhv.astype(F32), axis=0, keepdims=True)
        db1 = part if db1 is None else db1 + part

        @pl.when(j == 0)
        def _():
            acc[rows, :] = o
            dsec[rows, :] = ds

        @pl.when(j > 0)
        def _():
            acc[rows, :] += o
            dsec[rows, :] += ds

    db1_ref[...] = db1
    half = d // 2
    keep = pl.ds(pl.multiple_of(c * half, half), half)
    send = pl.ds(pl.multiple_of((1 - c) * half, half), half)
    pc = dw2_k_ref.shape[2]
    npc = w1_ref.shape[1] // pc
    g = dot(up_t[keep, :], act[...], NN).astype(BF)
    for p in range(npc):
        dw2_k_ref[p] = g[:, p * pc : (p + 1) * pc]
    g = dot(up_t[send, :], act[...], NN).astype(BF)
    for p in range(npc):
        dw2_s_ref[p] = g[:, p * pc : (p + 1) * pc]
    g = dot(sec_t[...], dh[...], NN).astype(BF).reshape(dw1_k_ref.shape)

    @pl.when(j < nj // 2)
    def _():
        dw1_s_ref[...] = g

    @pl.when(j >= nj // 2)
    def _():
        dw1_k_ref[...] = g

    @pl.when(j == nj - 1)
    def _():
        for t in range(tiles):
            rows = pl.ds(t * tm, tm)
            m = mid[rows, :]
            out_ref[rows, :] = (m + acc[rows, :] + b2_ref[...]).astype(BF)
            spread, r = stats(m)
            nv = spread * r
            dy = dsec[rows, :]
            dyg = dy * g2_ref[...]
            up = up_ref[rows, :].astype(F32)
            dm = up + r * (
                dyg
                - jnp.mean(dyg, axis=-1, keepdims=True)
                - nv * jnp.mean(dyg * nv, axis=-1, keepdims=True)
            )
            db = dm.astype(BF)
            dbr_ref[rows, :] = db
            do_ref[rows, :] = (dot(db, wo_ref[...], NT) * li_ref[rows, :]).astype(BF)
            vec_ref[0:1, :] += jnp.sum(db.astype(F32), axis=0, keepdims=True)
            vec_ref[1:2, :] += jnp.sum(dy * nv, axis=0, keepdims=True)
            vec_ref[2:3, :] += jnp.sum(dy, axis=0, keepdims=True)
            vec_ref[3:4, :] += jnp.sum(up, axis=0, keepdims=True)
            sec_t[:, rows] = mix_ref[rows, :].T
        g = dot(sec_t[...], dbr_ref[...], NN).astype(BF)
        left = g[:, :half].reshape(dwo_k_ref.shape)
        right = g[:, half:].reshape(dwo_k_ref.shape)

        @pl.when(c == 0)
        def _():
            dwo_k_ref[...] = left
            dwo_s_ref[...] = right

        @pl.when(c == 1)
        def _():
            dwo_k_ref[...] = right
            dwo_s_ref[...] = left


def mlp(core, x, mix, li, up, wo, bo, g2, s2, w1, b1, w2, b2, nv, fw=768, tm=512):
    n, d = x.shape
    ff = w1.shape[1]
    nj = ff // fw
    pc = ff // nv if ff // nv < fw else fw
    pieces = ff // pc
    h = nj // 2

    def full(*s):
        return pl.BlockSpec(s, lambda j, c: (0,) * len(s), pipeline_mode=pl.Buffered(1))

    def jj(j, c):
        return (j + (1 - c[0]) * h) % nj

    npc = fw // pc
    dr = d // nv
    piece = pl.BlockSpec((npc, d // 2, pc), lambda j, c: (jj(j, c), 0, 0))
    grid_spec = pltpu.PrefetchScalarGridSpec(
        num_scalar_prefetch=1,
        grid=(nj,),
        in_specs=[
            full(n, d), full(n, d), full(n, d), full(n, d), full(d, d), full(1, d), full(1, d), full(1, d),
            pl.BlockSpec((d, fw), lambda j, c: (0, jj(j, c))),
            pl.BlockSpec((1, fw), lambda j, c: (0, jj(j, c))),
            pl.BlockSpec((fw, d), lambda j, c: (jj(j, c), 0)),
            full(1, d),
        ],
        out_specs=[
            full(n, d), full(n, d), full(n, d), full(nv, dr, d // 2), full(nv, dr, d // 2),
            pl.BlockSpec((nv, dr, fw), lambda j, c: (0, 0, jnp.maximum(j - h, 0))),
            pl.BlockSpec((nv, dr, fw), lambda j, c: (0, 0, jnp.minimum(j, h - 1))),
            piece, piece, full(8, d),
            pl.BlockSpec((1, fw), lambda j, c: (0, jj(j, c))),
        ],
        scratch_shapes=[
            pltpu.VMEM((n, d), BF), pltpu.VMEM((d, n), BF), pltpu.VMEM((d, n), BF),
            pltpu.VMEM((n, d), F32), pltpu.VMEM((n, d), F32), pltpu.VMEM((n, d), F32),
            pltpu.VMEM((n, fw), BF), pltpu.VMEM((n, fw), BF),
        ],
    )
    return pl.pallas_call(
        functools.partial(mlp_kernel, tm=tm, nj=nj),
        grid_spec=grid_spec,
        out_shape=[
            shape((n, d)), shape((n, d)), shape((n, d)), shape((nv, dr, d // 2)), shape((nv, dr, d // 2)),
            shape((nv, dr, ff // 2)), shape((nv, dr, ff // 2)), shape((pieces, d // 2, pc)), shape((pieces, d // 2, pc)),
            shape((8, d), F32), shape((1, ff), F32),
        ],
        compiler_params=params(),
        cost_estimate=pl.CostEstimate(flops=24 * n * d * ff, bytes_accessed=8 * d * ff, transcendentals=0),
        name="mlp",
    )(core, x, mix, li, up, wo, bo, g2, s2, w1, b1, w2, b2)


def reflect_kernel(c_ref, q_ref, k_ref, v_ref, o_ref, do_ref, p_ref, ft_ref, dq_ref, dk_ref, dv_ref, gk_ref, gs_ref, ds_ref, *, tq):
    n = k_ref.shape[0]
    low = lax.broadcasted_iota(jnp.int32, (tq, PAIR), 1) < HEAD_DIM
    q_t = q_ref[...].T
    do_t = do_ref[...].T
    scale = HEAD_DIM**-0.5
    dks, dvs = [], []
    for a in range(2):
        for t in range(n // tq):
            rows = pl.ds(t * tq, tq)
            do = do_ref[rows, :]
            zero = jnp.zeros_like(do)
            doa = jnp.where(low, do, zero) if a == 0 else jnp.where(low, zero, do)
            delta = jnp.sum(doa.astype(F32) * o_ref[rows, :].astype(F32), axis=-1, keepdims=True)
            dp = dot(doa, v_ref[...], NT)
            ds = (p_ref[a, rows, :].astype(F32) * (dp - delta)).astype(BF)
            ds_ref[rows, :] = ds
            dq = (dot(ds, k_ref[...], NN) * scale).astype(BF)
            dq_ref[rows, :] = dq if a == 0 else jnp.where(low, dq_ref[rows, :], dq)
        part = slice(HEAD_DIM * a, HEAD_DIM * (a + 1))
        dvs.append(dot(do_t[part], p_ref[a], NN))
        dks.append(dot(q_t[part], ds_ref[...], NN) * scale)
    dv = jnp.concatenate(dvs, axis=0).astype(BF).T
    dk = jnp.concatenate(dks, axis=0).astype(BF).T
    dv_ref[...] = dv
    dk_ref[...] = dk
    g = dot(ft_ref[...], jnp.concatenate([dq_ref[...], dk, dv], axis=1), NN).astype(BF)
    nv, rows, wide = gk_ref.shape
    g = g.reshape(nv, 2, rows, wide)

    @pl.when(c_ref[0] == 0)
    def _():
        gk_ref[...] = g[:, 0]
        gs_ref[...] = g[:, 1]

    @pl.when(c_ref[0] == 1)
    def _():
        gk_ref[...] = g[:, 1]
        gs_ref[...] = g[:, 0]


def reflect(core, packed, o, do, p, first_t, nv, start, count):
    n, w = packed.shape
    d = w // 3
    hp = d // PAIR

    def cols(off):
        return pl.BlockSpec((n, PAIR), lambda h, c: (0, h + off))

    piece = pl.BlockSpec((nv, d // nv // 2, 3 * PAIR), lambda h, c: (0, 0, h))
    return pl.pallas_call(
        functools.partial(reflect_kernel, tq=256),
        grid_spec=pltpu.PrefetchScalarGridSpec(
            num_scalar_prefetch=1,
            grid=(count,),
            in_specs=[
                cols(start), cols(start + hp), cols(start + 2 * hp), cols(start), cols(start),
                pl.BlockSpec((2, n, n), lambda h, c: (h + start, 0, 0)),
                pl.BlockSpec((d, n), lambda h, c: (0, 0)),
            ],
            out_specs=[cols(0)] * 3 + [piece] * 2,
            scratch_shapes=[pltpu.VMEM((n, n), BF)],
        ),
        out_shape=[shape((n, count * PAIR))] * 3 + [shape((nv, d // nv // 2, 3 * PAIR * count))] * 2,
        compiler_params=params(),
        cost_estimate=pl.CostEstimate(flops=80 * n * n * PAIR * count, bytes_accessed=4 * n * n * count, transcendentals=0),
        name="reflect",
    )(core, packed, packed, packed, o, do, p, first_t)


def back_kernel(*refs, chunks):
    x_ref, dbr_ref, w_ref, g_ref = refs[:4]
    parts = refs[4 : 4 + 3 * chunks]
    tg_ref, vec_ref = refs[4 + 3 * chunks :]

    @pl.when(pl.program_id(0) == 0)
    def _():
        vec_ref[...] = jnp.zeros_like(vec_ref)

    d = x_ref.shape[1]
    cw = d // chunks
    dy = None
    for i in range(3 * chunks):
        which, chunk = i % 3, i // 3
        at = which * d + chunk * cw
        part = dot(parts[i][...], w_ref[:, at : at + cw], NT)
        dy = part if dy is None else dy + part
        row = {0: 2, 2: 3}.get(which)
        if row is not None:
            vec_ref[row : row + 1, chunk * cw : (chunk + 1) * cw] += jnp.sum(parts[i][...].astype(F32), axis=0, keepdims=True)
    spread, r = stats(x_ref[...].astype(F32))
    nv = spread * r
    dyg = dy * g_ref[...]
    dx = r * (dyg - jnp.mean(dyg, axis=-1, keepdims=True) - nv * jnp.mean(dyg * nv, axis=-1, keepdims=True))
    tg_ref[...] = (dbr_ref[...].astype(F32) + dx).astype(BF)
    vec_ref[0:1, :] += jnp.sum(dy * nv, axis=0, keepdims=True)
    vec_ref[1:2, :] += jnp.sum(dy, axis=0, keepdims=True)


def project_back(x, dbr, w, g, parts):
    n, d = x.shape
    tm = 256
    row = pl.BlockSpec((tm, d), lambda i: (i, 0))

    def full(*s):
        return pl.BlockSpec(s, lambda i: (0, 0))

    chunks = len(parts) // 3
    return pl.pallas_call(
        functools.partial(back_kernel, chunks=chunks),
        grid=(n // tm,),
        in_specs=[row, row, full(d, 3 * d), full(1, d)] + [pl.BlockSpec((tm, d // chunks), lambda i: (i, 0))] * (3 * chunks),
        out_specs=[row, full(8, d)],
        out_shape=[shape((n, d)), shape((8, d), F32)],
        compiler_params=params(),
        cost_estimate=pl.CostEstimate(flops=6 * n * d * d, bytes_accessed=16 * n * d, transcendentals=0),
        name="project_back",
    )(x, dbr, w, g, *parts)


def exchange(x, axis, by):
    count = lax.axis_size(axis)
    return lax.ppermute(x, axis, [(i, i ^ by) for i in range(count)])


def pick(x, index, axis=0):
    return lax.dynamic_index_in_dim(x, index, axis, keepdims=False)


def total(arrays, dtype=BF):
    s = arrays[0].astype(F32)
    for a in arrays[1:]:
        s = s + a.astype(F32)
    return s.astype(dtype)


def volume_sum(kept, sent, dtype=BF):
    position = lax.axis_index("vol")
    held = [kept, exchange(sent, "seq", 1)]
    count = lax.axis_size("vol")
    bit = 1
    while bit < count:
        split = [a.reshape((a.shape[0] // 2, 2) + a.shape[1:]) for a in held]
        mine = (position // bit) % 2
        received = exchange(total([pick(a, 1 - mine, 1) for a in split], dtype), "vol", bit)
        held = [pick(a, mine, 1) for a in split] + [received]
        bit *= 2
    mine = total([a[0] for a in held], dtype)
    mine = total([mine, exchange(mine, "seq", 2)], dtype)
    return mine, exchange(mine, "seq", 1)


def on_device(
    volume_slices, volume_owner, tokens, cotangent, attend_gain, attend_shift, input_weight, query_bias, value_bias,
    output_weight, output_bias, mixer_gain, mixer_shift, expand_weight, expand_bias, reduce_weight, reduce_bias,
):
    slices, rows, d = tokens.shape
    ff = expand_weight.shape[1]
    nv = lax.axis_size("vol")
    peers = lax.axis_size("seq")
    me = lax.axis_index("seq")
    core_id = me % 2
    core = core_id.astype(jnp.int32).reshape(1)
    load = jnp.sum(jnp.where(volume_owner == lax.axis_index("vol"), volume_slices, 0))
    line = lambda v: v.astype(F32).reshape(1, -1)

    def to_slice(x, k):
        part = pick(x, me ^ k)
        return part if k == 0 else exchange(part, "seq", k)

    live = (jnp.arange(slices) < load).astype(cotangent.dtype)
    near = jnp.concatenate([to_slice(tokens, 0), to_slice(tokens, 1)])
    far_parts = [to_slice(tokens, k) for k in range(2, peers)]
    far = jnp.concatenate(far_parts)
    n = rows * peers
    bias = jnp.concatenate([line(query_bias), jnp.zeros((1, d), F32), line(value_bias)], axis=1)
    gain, shift = line(attend_gain), line(attend_shift)
    made = project_in(near, 0, n, None, gain, shift, input_weight, bias)
    x, first_t, packed = project_in(far, near.shape[0], n, made, gain, shift, input_weight, bias)
    cotangent, _ = lax.optimization_barrier((cotangent, far_parts[-1]))
    upstream = jnp.concatenate([to_slice(cotangent * live[:, None, None], k) for k in range(peers)])

    mixed, inverse, weights = attend(packed)
    (out, d_branch, d_mixed, dwo_k, dwo_s, dw1_k, dw1_s, dw2_k, dw2_s, vec_mid, db1) = mlp(
        core, x, mixed, inverse, upstream, output_weight, line(output_bias), line(mixer_gain), line(mixer_shift),
        expand_weight, line(expand_bias), reduce_weight, line(reduce_bias), nv,
    )
    if dw2_k.shape[0] != nv:
        regroup = lambda a: a.reshape(a.shape[0], d // 2, -1, ff // nv).swapaxes(1, 2).reshape(nv, d // 2, ff // nv)
        dw2_k, dw2_s = regroup(dw2_k), regroup(dw2_s)
    sum_dw2 = volume_sum(dw2_k, dw2_s)
    sum_dw1 = volume_sum(dw1_k, dw1_s)
    sum_dwo = volume_sum(dwo_k, dwo_s)

    pairs = d // PAIR
    chunks = 3
    parts, sum_dwi = [], []
    for i in range(chunks):
        dq, dk, dv, gk, gs = reflect(core, packed, mixed, d_mixed, weights, first_t, nv, i * pairs // chunks, pairs // chunks)
        parts += [dq, dk, dv]
        sum_dwi.append(volume_sum(gk, gs))
    d_tokens, vec_end = project_back(x, d_branch, input_weight, gain, parts)

    def home(x, dtype, mask):
        result = jnp.zeros((slices, rows, d), dtype)
        for k in range(peers):
            part = x[k * rows : (k + 1) * rows]
            if k:
                part = exchange(part, "seq", k)
            if mask:
                part = part * pick(live, me ^ k)
            result = lax.dynamic_update_index_in_dim(result, part.astype(dtype), me ^ k, 0)
        return result

    block_out = home(out, BF, True)
    tokens_grad = home(d_tokens, F32, False)

    rows_of = jnp.concatenate([vec_end[:4], vec_mid[:4], db1.reshape(nv, ff // d, d // nv).swapaxes(0, 1).reshape(ff // d, d)])
    pieces = rows_of.reshape(-1, nv, d // nv).swapaxes(0, 1)
    half = pieces.shape[1] // 2
    small = volume_sum(
        lax.dynamic_slice_in_dim(pieces, core_id * half, half, 1),
        lax.dynamic_slice_in_dim(pieces, (1 - core_id) * half, half, 1), F32,
    )

    def join(pair, axis):
        a, b = pair
        first = jnp.where(core_id == 0, a, b).astype(F32)
        second = jnp.where(core_id == 0, b, a).astype(F32)
        return jnp.concatenate([first, second], axis)

    vectors = join(small, 0)
    reduce_grad = join(sum_dw2, 0).T
    expand_grad = join(sum_dw1, 1)
    output_grad = join(sum_dwo, 1)
    per = pairs // chunks
    input_grad = jnp.concatenate(
        [join(s, 0).reshape(d // nv, per, 3, PAIR).swapaxes(1, 2).reshape(d // nv, 3, per * PAIR) for s in sum_dwi], axis=2
    ).reshape(d // nv, 3 * d)
    return (
        block_out, tokens_grad, vectors[0], vectors[1], input_grad, vectors[2], vectors[3], output_grad, vectors[4],
        vectors[5], vectors[6], expand_grad, vectors[8:].reshape(-1), reduce_grad, vectors[7],
    )


def solution(mesh):
    rows = P("vol", "seq", None)
    return jax.shard_map(
        on_device,
        mesh=mesh,
        in_specs=(P(), P(), rows, rows) + (P(),) * 13,
        out_specs=(rows, rows, P("vol"), P("vol"), P("vol", None), P("vol"), P("vol"), P("vol", None), P("vol"), P("vol"),
                   P("vol"), P("vol", None), P("vol"), P("vol", None), P("vol")),
        check_vma=False,
    )
```

time: 959 us -> 417 us (0.43)
  waiting for transfers between devices: 453 us -> 121 us
  matrix products: 252 us -> 0 us
  Pallas kernels: 0 us -> 142 us
  other arithmetic: 120 us -> 42.9 us
  starting transfers between devices: 2.96 us -> 53.3 us
  local copies, waits for them, and re-layouts: 100 us -> 50.1 us
  between operations: 15.3 us -> 1.58 us
    reduce_scatter x4 -> x0, waiting for transfers between devices: 262 us -> none  [the longest x1 132 us: on_device(): lax.psum_scatter(expand_grad, 'vol', scatter_dimension=0, tiled=True)]
    dot_general x36 -> x0, matrix products: 252 us -> none  [the longest x4 35 us: reflect(): jnp.einsum('crhd,cshd->chrs', grad_heads, value_heads, preferred_element_...]
    pallas_call x0 -> x8, Pallas kernels: none -> 142 us  [the longest x1 56.4 us: mlp(): pl.pallas_call(functools.partial(mlp_kernel, tm=tm, nj=nj), grid_spec=gri...]
    convert_element_type x23 -> x31, other arithmetic: 72.1 us -> 17.9 us  [the longest x30 17.2 us: total(): return s.astype(dtype)]
    unnamed x7 -> x0, waiting for transfers between devices: 52.1 us -> none
    ppermute x7 -> x54, starting transfers between devices: 2.71 us -> 53.3 us  [exchange(): return lax.ppermute(x, axis, [(i, i ^ by) for i in range(count)])]
    reduce_sum x12 -> x1, other arithmetic: 42.2 us -> 1.31 us  [on_device(): jnp.sum(jnp.where(volume_owner == lax.axis_index('vol'), volume_slices, 0))]
    psum x1 -> x0, waiting for transfers between devices: 40.2 us -> none  [on_device(): lax.psum(parts[0].astype(jnp.bfloat16), 'seq').astype(jnp.float32)]
  transfers between devices with their start and end apart: 13 -> 54, of which waited for: 10 -> 26; matrix products, arithmetic and copies ran while one was open for 32% -> 21% of each run, Pallas kernels for 0% -> 10%
where the time goes in v1:
time: 417 us; the launch traced here: 410 us
  Pallas kernels  142 us (34%)
  waiting for transfers between devices  121 us (29%)
  starting transfers between devices  53.3 us (13%)
  local copies, waits for them, and re-layouts  50.1 us (12%)
  other arithmetic  42.9 us (10%)
    ppermute x54, waiting for transfers between devices, exchange(): return lax.ppermute(x, axis, [(i, i ^ by) for i in range(count)])  121 us
    pallas_call x1, Pallas kernels, mlp(): pl.pallas_call(functools.partial(mlp_kernel, tm=tm, nj=nj), grid_spec=gri...  56.4 us
    ppermute x54, starting transfers between devices, exchange(): return lax.ppermute(x, axis, [(i, i ^ by) for i in range(count)])  53.3 us
    pallas_call x3, Pallas kernels, reflect(): pl.pallas_call(functools.partial(reflect_kernel, tq=256), grid_spec=pltpu...  42.3 us
    pallas_call x1, Pallas kernels, attend(): pl.pallas_call(functools.partial(attend_kernel, tq=128), grid=(hp,), in_s...  21.2 us
    convert_element_type x30, other arithmetic, total(): return s.astype(dtype)  17.2 us
    dynamic_slice x17, local copies, waits for them, and re-layouts, pick(): return lax.dynamic_index_in_dim(x, index, axis, keepdims=False)  14.6 us
    pallas_call x2, Pallas kernels, project_in(): pl.pallas_call(in_kernel, grid=(rows // tm,), in_specs=in_specs, out_spec...  11.8 us
  transfers between devices with their start and end apart: 54, of which 26 were waited for; matrix products, arithmetic and copies ran while one was open for 21% of the time, Pallas kernels for 10%

profile of v1, /device:TPU:0, one launch (start us, length us, event | category | flops | bytes accessed | tf_op | source)
XLA Modules:
  0.0 410.1 jit_solution(16328289866367687339)
XLA Ops:
  23.8 5.9 %project_in.2 = (bf16[1024,768]{1,0:T(8,128)(2,1)}, bf16[768,1024]{1,0:T(8,128)(2,1)}, bf16[1024,2304]{1,0:T(8,128)(2,1)}) custom-call(bf16[512,768]{1,0:T(8,128)(2,1)} %pad_maximum_fusion.2.x_ref, f32[1,768]{1,0:T(1,128)} %reshape.973.g_ref.refs_3_, f32[1,768]{1,0:T(1,128)} %reshape.975.b_ref, bf16[768,2304]{1,0:T(8,128)(2,1)} %refs_2_.1, ...), custom_call_target="tpu_custom_call" | custom-call | flops 1811939328 | bytes 8257536 | tf_op jit(solution)/shard_map/project_in/pallas_call | solution.py:83
  30.7 5.8 %project_in.3 = (bf16[1024,768]{1,0:T(8,128)(2,1)}, bf16[768,1024]{1,0:T(8,128)(2,1)}, bf16[1024,2304]{1,0:T(8,128)(2,1)}) custom-call(bf16[512,768]{1,0:T(8,128)(2,1)} %pad_maximum_fusion.1.x_ref, f32[1,768]{1,0:T(1,128)} %reshape.973.g_ref.refs_3_, f32[1,768]{1,0:T(1,128)} %reshape.975.b_ref, ...), custom_call_target="tpu_custom_call", output_to_operand_aliasing={{0}: (5, {}), {1}: (6, {}), {2}: (7, {})} | custom-call | flops 1811939328 | bytes 8257536 | tf_op jit(solution)/shard_map/project_in/pallas_call | solution.py:83
  36.5 21.2 %attend.1 = (bf16[1024,768]{1,0:T(8,128)(2,1)}, f32[1024,768]{1,0:T(8,128)}, bf16[12,1024,1024]{2,1,0:T(8,128)(2,1)}) custom-call(bf16[1024,2304]{1,0:T(8,128)(2,1)} %get-tuple-element.57.q_ref.k_ref.v_ref, bf16[1024,2304]{1,0:T(8,128)(2,1)} %get-tuple-element.57.q_ref.k_ref.v_ref, bf16[1024,2304]{1,0:T(8,128)(2,1)} %get-tuple-element.57.q_ref.k_ref.v_ref), custom_call_target="tpu_custom_call" | custom-call | flops 12884901888 | bytes 25165824 | tf_op jit(solution)/shard_map/attend/pallas_call | solution.py:131
  59.1 56.4 %mlp.1 = (bf16[1024,768]{1,0:T(8,128)(2,1)}, bf16[1024,768]{1,0:T(8,128)(2,1)}, bf16[1024,768]{1,0:T(8,128)(2,1)}, bf16[8,96,384]{2,1,0:T(8,128)(2,1)}, bf16[8,9...) custom-call(s32[1]{0:T(128)} %bitcast.c_ref, ...), custom_call_target="tpu_custom_call" | custom-call | flops 57982058496 | bytes 18874368 | tf_op jit(solution)/shard_map/mlp/pallas_call | solution.py:293
  115.5 14.1 %reflect.3 = (bf16[1024,256]{1,0:T(8,128)(2,1)}, bf16[1024,256]{1,0:T(8,128)(2,1)}, bf16[1024,256]{1,0:T(8,128)(2,1)}, bf16[8,48,768]{2,1,0:T(8,128)(2,1)}, bf16[8,48,768]{2,1,0:T(8,128)(2,1)}) custom-call(s32[1]{0:T(128)} %bitcast.c_ref, bf16[1024,2304]{1,0:T(8,128)(2,1)} %get-tuple-element.57.q_ref.k_ref.v_ref, ...), custom_call_target="tpu_custom_call" | custom-call | flops 21474836480 | bytes 8388608 | tf_op jit(solution)/shard_map/reflect/pallas_call | solution.py:357
  129.5 14.1 %reflect.4 = (bf16[1024,256]{1,0:T(8,128)(2,1)}, bf16[1024,256]{1,0:T(8,128)(2,1)}, bf16[1024,256]{1,0:T(8,128)(2,1)}, bf16[8,48,768]{2,1,0:T(8,128)(2,1)}, bf16[8,48,768]{2,1,0:T(8,128)(2,1)}) custom-call(s32[1]{0:T(128)} %bitcast.c_ref, bf16[1024,2304]{1,0:T(8,128)(2,1)} %get-tuple-element.57.q_ref.k_ref.v_ref, ...), custom_call_target="tpu_custom_call" | custom-call | flops 21474836480 | bytes 8388608 | tf_op jit(solution)/shard_map/reflect/pallas_call | solution.py:357
  143.6 14.1 %reflect.5 = (bf16[1024,256]{1,0:T(8,128)(2,1)}, bf16[1024,256]{1,0:T(8,128)(2,1)}, bf16[1024,256]{1,0:T(8,128)(2,1)}, bf16[8,48,768]{2,1,0:T(8,128)(2,1)}, bf16[8,48,768]{2,1,0:T(8,128)(2,1)}) custom-call(s32[1]{0:T(128)} %bitcast.c_ref, bf16[1024,2304]{1,0:T(8,128)(2,1)} %get-tuple-element.57.q_ref.k_ref.v_ref, ...), custom_call_target="tpu_custom_call" | custom-call | flops 21474836480 | bytes 8388608 | tf_op jit(solution)/shard_map/reflect/pallas_call | solution.py:357
  160.6 10.0 %project_back.1 = (bf16[1024,768]{1,0:T(8,128)(2,1)}, f32[8,768]{1,0:T(8,128)}) custom-call(bf16[1024,768]{1,0:T(8,128)(2,1)} %get-tuple-element.56.x_ref.refs_0_, bf16[1024,768]{1,0:T(8,128)(2,1)} %get-tuple-element.62.refs_1_, bf16[768,2304]{1,0:T(8,128)(2,1)} %refs_2_.1, f32[1,768]{1,0:T(1,128)} %reshape.973.g_ref.refs_3_, ...), custom_call_target="tpu_custom_call" | custom-call | flops 3623878656 | bytes 12582912 | tf_op jit(solution)/shard_map/project_back/pallas_call | solution.py:415
  210.2 6.7 %collective-permute-done.10 = bf16[256,768]{1,0:T(8,128)(2,1)} collective-permute-done((bf16[256,768]{1,0:T(8,128)(2,1)}, bf16[256,768]{1,0:T(8,128)(2,1)}, u32[]{:S(2)}, u32[]{:S(2)}) %collective-permute-start.10) | collective-permute-done | bytes 393248 | tf_op jit(solution)/shard_map/ppermute | solution.py:429
  218.8 4.9 %collective-permute-done.11 = bf16[256,768]{1,0:T(8,128)(2,1)S(1)} collective-permute-done((bf16[256,768]{1,0:T(8,128)(2,1)}, bf16[256,768]{1,0:T(8,128)(2,1)S(1)}, u32[]{:S(2)}, u32[]{:S(2)}) %collective-permute-start.11) | collective-permute-done | bytes 393248 | tf_op jit(solution)/shard_map/ppermute | solution.py:429
  227.2 8.4 %collective-permute-done.7 = bf16[256,768]{1,0:T(8,128)(2,1)S(1)} collective-permute-done((bf16[256,768]{1,0:T(8,128)(2,1)S(1)}, bf16[256,768]{1,0:T(8,128)(2,1)S(1)}, u32[]{:S(2)}, u32[]{:S(2)}) %collective-permute-start.7) | collective-permute-done | bytes 393248 | tf_op jit(solution)/shard_map/ppermute | solution.py:429
  236.3 6.9 %collective-permute-done.8 = bf16[256,768]{1,0:T(8,128)(2,1)S(1)} collective-permute-done((bf16[256,768]{1,0:T(8,128)(2,1)S(1)}, bf16[256,768]{1,0:T(8,128)(2,1)S(1)}, u32[]{:S(2)}, u32[]{:S(2)}) %collective-permute-start.8) | collective-permute-done | bytes 393248 | tf_op jit(solution)/shard_map/ppermute | solution.py:429
  257.5 4.5 %collective-permute-done.19 = bf16[4,48,768]{2,1,0:T(8,128)(2,1)S(1)} collective-permute-done((bf16[4,48,768]{2,1,0:T(8,128)(2,1)S(1)}, bf16[4,48,768]{2,1,0:T(8,128)(2,1)S(1)}, u32[]{:S(2)}, u32[]{:S(2)}) %collective-permute-start.19) | collective-permute-done | bytes 294944 | tf_op jit(solution)/shard_map/ppermute | solution.py:429
  263.8 4.5 %collective-permute-done.25 = bf16[4,48,768]{2,1,0:T(8,128)(2,1)S(1)} collective-permute-done((bf16[4,48,768]{2,1,0:T(8,128)(2,1)S(1)}, bf16[4,48,768]{2,1,0:T(8,128)(2,1)S(1)}, u32[]{:S(2)}, u32[]{:S(2)}) %collective-permute-start.25) | collective-permute-done | bytes 294944 | tf_op jit(solution)/shard_map/ppermute | solution.py:429
  270.2 3.8 collective-permute-done.31
  279.1 4.0 collective-permute-done.26
  287.9 4.0 collective-permute-done.21
  311.0 3.0 constant_dynamic-slice_fusion
  318.5 14.3 %collective-permute-done.49 = bf16[4,384,384]{2,1,0:T(8,128)(2,1)} collective-permute-done((bf16[4,384,384]{2,1,0:T(8,128)(2,1)}, bf16[4,384,384]{2,1,0:T(8,128)(2,1)}, u32[]{:S(2)}, u32[]{:S(2)}) %collective-permute-start.49) | collective-permute-done | bytes 1179680 | tf_op jit(solution)/shard_map/ppermute | solution.py:429
  337.5 20.2 %collective-permute-done.43 = bf16[4,96,1536]{2,1,0:T(8,128)(2,1)} collective-permute-done((bf16[4,96,1536]{2,1,0:T(8,128)(2,1)}, bf16[4,96,1536]{2,1,0:T(8,128)(2,1)}, u32[]{:S(2)}, u32[]{:S(2)}) %collective-permute-start.43) | collective-permute-done | bytes 1179680 | tf_op jit(solution)/shard_map/ppermute | solution.py:429
  368.7 3.2 collective-permute-start.51
  372.0 6.6 %collective-permute-done.44 = bf16[2,96,1536]{2,1,0:T(8,128)(2,1)} collective-permute-done((bf16[2,96,1536]{2,1,0:T(8,128)(2,1)}, bf16[2,96,1536]{2,1,0:T(8,128)(2,1)}, u32[]{:S(2)}, u32[]{:S(2)}) %collective-permute-start.44) | collective-permute-done | bytes 589856 | tf_op jit(solution)/shard_map/ppermute | solution.py:429
  380.0 12.6 %collective-permute-done.51 = bf16[1,384,384]{1,2,0:T(8,128)(2,1)S(1)} collective-permute-done((bf16[1,384,384]{1,2,0:T(8,128)(2,1)S(1)}, bf16[1,384,384]{1,2,0:T(8,128)(2,1)S(1)}, u32[]{:S(2)}, u32[]{:S(2)}) %collective-permute-start.51) | collective-permute-done | bytes 294944 | tf_op jit(solution)/shard_map/ppermute | solution.py:429
  402.3 4.6 %collective-permute-done.46 = bf16[96,1536]{1,0:T(8,128)(2,1)S(1)} collective-permute-done((bf16[96,1536]{1,0:T(8,128)(2,1)S(1)}, bf16[96,1536]{1,0:T(8,128)(2,1)S(1)}, u32[]{:S(2)}, u32[]{:S(2)}) %collective-permute-start.46) | collective-permute-done | bytes 294944 | tf_op jit(solution)/shard_map/ppermute | solution.py:429
  (279 shorter events, 154.7 us)
Async XLA Ops:
  3.2 19.7 %collective-permute-start.2 = (bf16[256,768]{1,0:T(8,128)(2,1)}, bf16[256,768]{1,0:T(8,128)(2,1)S(1)}, u32[]{:S(2)}, u32[]{:S(2)}) collective-permute-start(bf16[256,768]{1,0:T(8,128)(2,1)} %get-tuple-element.104), channel_id=1, source_target_pairs={{0,1},{1,0},{2,3},{3,2},{4,5},{5,4},{6,7},{7,6},{8,9},{9,8},{10,11... | collective-permute-start | bytes 1179656 | tf_op jit(solution)/shard_map/ppermute | solution.py:429
  3.6 15.9 %collective-permute-start.1 = (bf16[256,768]{1,0:T(8,128)(2,1)}, bf16[256,768]{1,0:T(8,128)(2,1)S(1)}, u32[]{:S(2)}, u32[]{:S(2)}) collective-permute-start(bf16[256,768]{1,0:T(8,128)(2,1)} %get-tuple-element.102), channel_id=1, source_target_pairs={{0,3},{1,2},{2,1},{3,0},{4,7},{5,6},{6,5},{7,4},{8,11},{9,10},{10,... | collective-permute-start | bytes 1179656 | tf_op jit(solution)/shard_map/ppermute | solution.py:429
  6.2 23.6 %collective-permute-start = (bf16[256,768]{1,0:T(8,128)(2,1)S(1)}, bf16[256,768]{1,0:T(8,128)(2,1)S(1)}, u32[]{:S(2)}, u32[]{:S(2)}) collective-permute-start(bf16[256,768]{1,0:T(8,128)(2,1)S(1)} %get-tuple-element.103), channel_id=1, source_target_pairs={{0,2},{1,3},{2,0},{3,1},{4,6},{5,7},{6,4},{7,5},{8,10},{9,11},{10,... | collective-permute-start | bytes 1179656 | tf_op jit(solution)/shard_map/ppermute | solution.py:429
  20.7 37.0 %collective-permute-start.3 = (bf16[256,768]{1,0:T(8,128)(2,1)}, bf16[256,768]{1,0:T(8,128)(2,1)S(1)}, u32[]{:S(2)}, u32[]{:S(2)}) collective-permute-start(bf16[256,768]{1,0:T(8,128)(2,1)} %get-tuple-element.100), channel_id=1, source_target_pairs={{0,1},{1,0},{2,3},{3,2},{4,5},{5,4},{6,7},{7,6},{8,9},{9,8},{10,11... | collective-permute-start | bytes 1179656 | tf_op jit(solution)/shard_map/ppermute | solution.py:429
  20.9 36.9 %collective-permute-start.4 = (bf16[256,768]{1,0:T(8,128)(2,1)}, bf16[256,768]{1,0:T(8,128)(2,1)S(1)}, u32[]{:S(2)}, u32[]{:S(2)}) collective-permute-start(bf16[256,768]{1,0:T(8,128)(2,1)} %get-tuple-element.99), channel_id=1, source_target_pairs={{0,2},{1,3},{2,0},{3,1},{4,6},{5,7},{6,4},{7,5},{8,10},{9,11},{10,... | collective-permute-start | bytes 1179656 | tf_op jit(solution)/shard_map/ppermute | solution.py:429
  22.7 35.0 %collective-permute-start.5 = (bf16[256,768]{1,0:T(8,128)(2,1)S(1)}, bf16[256,768]{1,0:T(8,128)(2,1)S(1)}, u32[]{:S(2)}, u32[]{:S(2)}) collective-permute-start(bf16[256,768]{1,0:T(8,128)(2,1)S(1)} %get-tuple-element.98), channel_id=1, source_target_pairs={{0,3},{1,2},{2,1},{3,0},{4,7},{5,6},{6,5},{7,4},{8,11},{9,10},{10,... | collective-permute-start | bytes 1179656 | tf_op jit(solution)/shard_map/ppermute | solution.py:429
  157.7 144.1 %collective-permute-start.48 = (bf16[8,384,384]{2,1,0:T(8,128)(2,1)}, bf16[8,384,384]{2,1,0:T(8,128)(2,1)S(1)}, u32[]{:S(2)}, u32[]{:S(2)}) collective-permute-start(bf16[8,384,384]{2,1,0:T(8,128)(2,1)} %get-tuple-element.90), channel_id=1, source_target_pairs={{0,1},{1,0},{2,3},{3,2},{4,5},{5,4},{6,7},{7,6},{8,9},{9,8},{10,11... | collective-permute-start | bytes 7077896 | tf_op jit(solution)/shard_map/ppermute | solution.py:429
  157.9 86.2 %collective-permute-start.36 = (bf16[8,96,384]{2,1,0:T(8,128)(2,1)}, bf16[8,96,384]{2,1,0:T(8,128)(2,1)}, u32[]{:S(2)}, u32[]{:S(2)}) collective-permute-start(bf16[8,96,384]{2,1,0:T(8,128)(2,1)} %get-tuple-element.86), channel_id=1, source_target_pairs={{0,1},{1,0},{2,3},{3,2},{4,5},{5,4},{6,7},{7,6},{8,9},{9,8},{10,11... | collective-permute-start | bytes 1769480 | tf_op jit(solution)/shard_map/ppermute | solution.py:429
  160.4 85.3 %collective-permute-start.18 = (bf16[8,48,768]{2,1,0:T(8,128)(2,1)}, bf16[8,48,768]{2,1,0:T(8,128)(2,1)}, u32[]{:S(2)}, u32[]{:S(2)}) collective-permute-start(bf16[8,48,768]{2,1,0:T(8,128)(2,1)} %get-tuple-element.80), channel_id=1, source_target_pairs={{0,1},{1,0},{2,3},{3,2},{4,5},{5,4},{6,7},{7,6},{8,9},{9,8},{10,11... | collective-permute-start | bytes 1769480 | tf_op jit(solution)/shard_map/ppermute | solution.py:429
  208.1 15.6 %collective-permute-start.11 = (bf16[256,768]{1,0:T(8,128)(2,1)}, bf16[256,768]{1,0:T(8,128)(2,1)S(1)}, u32[]{:S(2)}, u32[]{:S(2)}) collective-permute-start(bf16[256,768]{1,0:T(8,128)(2,1)} %get-tuple-element.91), channel_id=1, source_target_pairs={{0,3},{1,2},{2,1},{3,0},{4,7},{5,6},{6,5},{7,4},{8,11},{9,10},{10,... | collective-permute-start | bytes 1179656 | tf_op jit(solution)/shard_map/ppermute | solution.py:429
  226.1 17.1 %collective-permute-start.8 = (bf16[256,768]{1,0:T(8,128)(2,1)S(1)}, bf16[256,768]{1,0:T(8,128)(2,1)S(1)}, u32[]{:S(2)}, u32[]{:S(2)}) collective-permute-start(bf16[256,768]{1,0:T(8,128)(2,1)S(1)} %copy-done.25), channel_id=1, source_target_pairs={{0,3},{1,2},{2,1},{3,0},{4,7},{5,6},{6,5},{7,4},{8,11},{9,10},{10,... | collective-permute-start | bytes 1179656 | tf_op jit(solution)/shard_map/ppermute | solution.py:429
  244.2 59.5 %collective-permute-start.42 = (bf16[8,96,1536]{2,1,0:T(8,128)(2,1)S(1)}, bf16[8,96,1536]{2,1,0:T(8,128)(2,1)S(1)}, u32[]{:S(2)}, u32[]{:S(2)}) collective-permute-start(bf16[8,96,1536]{2,1,0:T(8,128)(2,1)S(1)} %copy-done.30), channel_id=1, source_target_pairs={{0,1},{1,0},{2,3},{3,2},{4,5},{5,4},{6,7},{7,6},{8,9},{9,8},{10,11... | collective-permute-start | bytes 7077896 | tf_op jit(solution)/shard_map/ppermute | solution.py:429
  248.6 13.4 %collective-permute-start.19 = (bf16[4,48,768]{2,1,0:T(8,128)(2,1)S(1)}, bf16[4,48,768]{2,1,0:T(8,128)(2,1)S(1)}, u32[]{:S(2)}, u32[]{:S(2)}) collective-permute-start(bf16[4,48,768]{2,1,0:T(8,128)(2,1)S(1)} %fusion.8), channel_id=1, source_target_pairs={{0,4},{4,0},{8,12},{12,8},{16,20},{20,16},{24,28},{28,24},{1,5},{5... | collective-permute-start | bytes 884744 | tf_op jit(solution)/shard_map/ppermute | solution.py:429
  249.0 19.2 %collective-permute-start.25 = (bf16[4,48,768]{2,1,0:T(8,128)(2,1)S(1)}, bf16[4,48,768]{2,1,0:T(8,128)(2,1)S(1)}, u32[]{:S(2)}, u32[]{:S(2)}) collective-permute-start(bf16[4,48,768]{2,1,0:T(8,128)(2,1)S(1)} %fusion.9), channel_id=1, source_target_pairs={{0,4},{4,0},{8,12},{12,8},{16,20},{20,16},{24,28},{28,24},{1,5},{5... | collective-permute-start | bytes 884744 | tf_op jit(solution)/shard_map/ppermute | solution.py:429
  255.6 18.3 %collective-permute-start.31 = (bf16[4,48,768]{2,1,0:T(8,128)(2,1)S(1)}, bf16[4,48,768]{2,1,0:T(8,128)(2,1)S(1)}, u32[]{:S(2)}, u32[]{:S(2)}) collective-permute-start(bf16[4,48,768]{2,1,0:T(8,128)(2,1)S(1)} %fusion.10), channel_id=1, source_target_pairs={{0,4},{4,0},{8,12},{12,8},{16,20},{20,16},{24,28},{28,24},{1,5},{5... | collective-permute-start | bytes 884744 | tf_op jit(solution)/shard_map/ppermute | solution.py:429
  262.0 13.9 %collective-permute-start.38 = (bf16[2,96,384]{2,1,0:T(8,128)(2,1)S(1)}, bf16[2,96,384]{2,1,0:T(8,128)(2,1)S(1)}, u32[]{:S(2)}, u32[]{:S(2)}) collective-permute-start(bf16[2,96,384]{2,1,0:T(8,128)(2,1)S(1)} %fusion.15), channel_id=1, source_target_pairs={{0,8},{4,12},{8,0},{12,4},{16,24},{20,28},{24,16},{28,20},{1,9},{5... | collective-permute-start | bytes 442376 | tf_op jit(solution)/shard_map/ppermute | solution.py:429
  299.2 67.2 %collective-permute-start.41 = (bf16[96,384]{1,0:T(8,128)(2,1)}, bf16[96,384]{1,0:T(8,128)(2,1)}, u32[]{:S(2)}, u32[]{:S(2)}) collective-permute-start(bf16[96,384]{1,0:T(8,128)(2,1)} %add_convert_fusion.14), channel_id=1, source_target_pairs={{0,1},{1,0},{2,3},{3,2},{4,5},{5,4},{6,7},{7,6},{8,9},{9,8},{10,11... | collective-permute-start | bytes 221192 | tf_op jit(solution)/shard_map/ppermute | solution.py:429
  301.9 57.9 %collective-permute-start.35 = (bf16[48,768]{1,0:T(8,128)(2,1)}, bf16[48,768]{1,0:T(8,128)(2,1)}, u32[]{:S(2)}, u32[]{:S(2)}) collective-permute-start(bf16[48,768]{1,0:T(8,128)(2,1)} %add_convert_fusion.15), channel_id=1, source_target_pairs={{0,1},{1,0},{2,3},{3,2},{4,5},{5,4},{6,7},{7,6},{8,9},{9,8},{10,11... | collective-permute-start | bytes 221192 | tf_op jit(solution)/shard_map/ppermute | solution.py:429
  303.7 29.1 %collective-permute-start.49 = (bf16[4,384,384]{2,1,0:T(8,128)(2,1)}, bf16[4,384,384]{2,1,0:T(8,128)(2,1)}, u32[]{:S(2)}, u32[]{:S(2)}) collective-permute-start(bf16[4,384,384]{2,1,0:T(8,128)(2,1)} %fusion.1), channel_id=1, source_target_pairs={{0,4},{4,0},{8,12},{12,8},{16,20},{20,16},{24,28},{28,24},{1,5},{5... | collective-permute-start | bytes 3538952 | tf_op jit(solution)/shard_map/ppermute | solution.py:429
  306.9 50.8 %collective-permute-start.43 = (bf16[4,96,1536]{2,1,0:T(8,128)(2,1)}, bf16[4,96,1536]{2,1,0:T(8,128)(2,1)}, u32[]{:S(2)}, u32[]{:S(2)}) collective-permute-start(bf16[4,96,1536]{2,1,0:T(8,128)(2,1)} %fusion), channel_id=1, source_target_pairs={{0,4},{4,0},{8,12},{12,8},{16,20},{20,16},{24,28},{28,24},{1,5},{5... | collective-permute-start | bytes 3538952 | tf_op jit(solution)/shard_map/ppermute | solution.py:429
  337.5 29.9 %collective-permute-start.50 = (bf16[2,384,384]{1,2,0:T(8,128)(2,1)}, bf16[2,384,384]{1,2,0:T(8,128)(2,1)}, u32[]{:S(2)}, u32[]{:S(2)}) collective-permute-start(bf16[2,384,384]{1,2,0:T(8,128)(2,1)} %fusion.3), channel_id=1, source_target_pairs={{0,8},{4,12},{8,0},{12,4},{16,24},{20,28},{24,16},{28,20},{1,9},{5... | collective-permute-start | bytes 1769480 | tf_op jit(solution)/shard_map/ppermute | solution.py:429
  359.8 18.8 %collective-permute-start.44 = (bf16[2,96,1536]{2,1,0:T(8,128)(2,1)}, bf16[2,96,1536]{2,1,0:T(8,128)(2,1)}, u32[]{:S(2)}, u32[]{:S(2)}) collective-permute-start(bf16[2,96,1536]{2,1,0:T(8,128)(2,1)} %fusion.2), channel_id=1, source_target_pairs={{0,8},{4,12},{8,0},{12,4},{16,24},{20,28},{24,16},{28,20},{1,9},{5... | collective-permute-start | bytes 1769480 | tf_op jit(solution)/shard_map/ppermute | solution.py:429
  368.7 23.8 %collective-permute-start.51 = (bf16[1,384,384]{1,2,0:T(8,128)(2,1)S(1)}, bf16[1,384,384]{1,2,0:T(8,128)(2,1)S(1)}, u32[]{:S(2)}, u32[]{:S(2)}) collective-permute-start(bf16[1,384,384]{1,2,0:T(8,128)(2,1)S(1)} %fusion.6), channel_id=1, source_target_pairs={{0,16},{4,20},{8,24},{12,28},{16,0},{20,4},{24,8},{28,12},{1,17},{... | collective-permute-start | bytes 884744 | tf_op jit(solution)/shard_map/ppermute | solution.py:429
  379.8 17.7 %collective-permute-start.45 = (bf16[1,96,1536]{2,1,0:T(8,128)(2,1)S(1)}, bf16[1,96,1536]{2,1,0:T(8,128)(2,1)S(1)}, u32[]{:S(2)}, u32[]{:S(2)}) collective-permute-start(bf16[1,96,1536]{2,1,0:T(8,128)(2,1)S(1)} %fusion.7), channel_id=1, source_target_pairs={{0,16},{4,20},{8,24},{12,28},{16,0},{20,4},{24,8},{28,12},{1,17},{... | collective-permute-start | bytes 884744 | tf_op jit(solution)/shard_map/ppermute | solution.py:429
  (62 other events, 626.9 us)
